TPU v7x, 32 devices: a whole 2x2x4 slice. The times are simulated.
32 devices in a mesh: groups: 2 (over x), blk: 16 (over z, y, core).
Axes of the slice: x: 2, y: 2, z: 4, core: 2. Of those that a mesh axis runs over, the one named last changes fastest.
Arguments:
- projections: bfloat16 [2, 512, 8192], P(None, ('groups', 'blk')), parts along dimension 1, may hold values from -12 to 12
- images: bfloat16 [64, 8192], P(('groups', 'blk')), parts along dimension 0, may hold values from -16 to 16, as said below
- ctf_group: int32 [64], P(('groups', 'blk')), parts along dimension 0, may hold values from 0 to 15
- shift_offsets: int32 [64, 9, 2], P(('groups', 'blk')), parts along dimension 0, may hold values from -8 to 8
- shell_limit: int32 [64], P(('groups', 'blk')), parts along dimension 0, may hold values from 16 to 63
- ctf_table: float32 [32, 4096], P('groups'), parts along dimension 0, may hold values from -1 to 1
- noise_weight: float32 [32, 4096], P('groups'), parts along dimension 0, may hold values from 0.25 to 4
Outputs:
- slices: float32 [2, 512, 8192], P(None, ('groups', 'blk')), parts along dimension 1
- best_posterior: float32 [64], P(('groups', 'blk')), parts along dimension 0
- log_total: float32 [64], P(('groups', 'blk')), parts along dimension 0
There are 2 independent parts, one for each index of `groups`. A program takes and returns all parts, laid end to end along the dimension named above; each array names one. Nothing has to cross between parts.
Inputs may be any that keep to these rules, and one draw needn't show every extreme that they name: `images`: image coefficients.
All inputs are finite; a program needn't handle non-finite values.
Results may differ from a plain program's by a relative error of at most 0.006.
Values may be sent and summed in bfloat16 or wider, within the bound.
No kernel may reach another device: no remote copies, remote signals or barrier semaphores. Data moves between devices by JAX's collectives and lax.ppermute only.
A program may use at most 128 MiB of HBM per device.

v0:
```python
import math
import jax
import jax.numpy as jnp
from jax import lax
from jax.sharding import PartitionSpec as P

KY = 64
IMG = 256


def combined_all(value, axis, join):
    pieces = jax.tree.map(lambda part: lax.all_gather(part, axis), value)
    head = jax.tree.map(lambda part: part[0], pieces)
    tail = jax.tree.map(lambda part: part[1:], pieces)
    so_far, _ = lax.scan(lambda so_far, section: (join(so_far, section), None), head, tail)
    return so_far


def frequencies(half_width):
    positions = jnp.arange(half_width, dtype=jnp.int32)
    return (positions // KY, positions % KY - KY // 2)


def shift_factors(offsets, half_width):
    row_count = offsets.shape[0]
    shift_count = offsets.shape[1]
    row_freq = jnp.arange(half_width // KY, dtype=jnp.int32)
    col_freq = jnp.arange(KY, dtype=jnp.int32) - KY // 2
    turns_x = row_freq[None, None, :] * offsets[:, :, 0:1] % IMG
    turns_y = col_freq[None, None, :] * offsets[:, :, 1:2] % IMG
    angle_x = turns_x.astype(jnp.float32) * (2.0 * math.pi / IMG)
    angle_y = turns_y.astype(jnp.float32) * (2.0 * math.pi / IMG)
    cosine_x = jnp.cos(angle_x)[:, :, :, None]
    sine_x = jnp.sin(angle_x)[:, :, :, None]
    cosine_y = jnp.cos(angle_y)[:, :, None, :]
    sine_y = jnp.sin(angle_y)[:, :, None, :]
    cosine = cosine_x * cosine_y - sine_x * sine_y
    sine_part = sine_x * cosine_y + cosine_x * sine_y
    return (
        cosine.reshape(row_count, shift_count, half_width),
        sine_part.reshape(row_count, shift_count, half_width),
    )


def particle_terms(image_rows, ctf_rows, weight_rows, offsets, limits, freq_x, freq_y):
    half_width = image_rows.shape[1] // 2
    image_real = image_rows[:, :half_width].astype(jnp.float32)
    image_imag = image_rows[:, half_width:].astype(jnp.float32)
    radius_sq = freq_x * freq_x + freq_y * freq_y
    inside = (radius_sq[None, :] < (limits * limits)[:, None]).astype(jnp.float32)
    masked_weight = inside * weight_rows
    ctf_weight = masked_weight * ctf_rows
    norm_term = jnp.sum(masked_weight * (image_real * image_real + image_imag * image_imag), axis=1)
    quad_weight = ctf_weight * ctf_rows
    cosine, sine_part = shift_factors(offsets, half_width)
    shift_real = image_real[:, None, :] * cosine + image_imag[:, None, :] * sine_part
    shift_imag = image_imag[:, None, :] * cosine - image_real[:, None, :] * sine_part
    weighted = jnp.concatenate(
        [ctf_weight[:, None, :] * shift_real, ctf_weight[:, None, :] * shift_imag], axis=2
    ).astype(jnp.bfloat16)
    return (weighted, norm_term, quad_weight)


def combine_lse(first, second):
    score_top = jnp.maximum(first[0], second[0])
    exp_total = first[1] * jnp.exp(first[0] - score_top) + second[1] * jnp.exp(
        second[0] - score_top
    )
    return (score_top, exp_total)


def block_shape(row_count):
    return 64 if row_count % 64 == 0 else row_count


def split_rows(members, block_rows):
    return tuple(
        (
            member.reshape((member.shape[0] // block_rows, block_rows) + member.shape[1:])
            for member in members
        )
    )


def local(projections, images, ctf_group, shift_offsets, shell_limit, ctf_table, noise_weight):
    batch_count, orient_dev, full_width = projections.shape
    half_width = full_width // 2
    candidates = batch_count * orient_dev
    flat_proj = projections.reshape(candidates, full_width)
    proj_real = flat_proj[:, :half_width].astype(jnp.float32)
    proj_imag = flat_proj[:, half_width:].astype(jnp.float32)
    proj_power = proj_real * proj_real + proj_imag * proj_imag
    freq_x, freq_y = frequencies(half_width)
    score_scale = 0.5 / math.sqrt(half_width)
    group_count = ctf_table.shape[0]
    particles_dev = images.shape[0]

    def block_terms(members):
        image_rows, groups, offsets, limits = members
        one_hot = (groups[:, None] == jnp.arange(group_count, dtype=jnp.int32)[None, :]).astype(
            jnp.float32
        )
        ctf_rows = jnp.dot(
            one_hot, ctf_table, precision=lax.Precision.HIGHEST, preferred_element_type=jnp.float32
        )
        weight_rows = jnp.dot(
            one_hot,
            noise_weight,
            precision=lax.Precision.HIGHEST,
            preferred_element_type=jnp.float32,
        )
        return particle_terms(image_rows, ctf_rows, weight_rows, offsets, limits, freq_x, freq_y)

    def score_block(members):
        weighted, norm_term, quad_weight = block_terms(members)
        cross_term = lax.dot_general(
            weighted, flat_proj, (((2,), (1,)), ((), ())), preferred_element_type=jnp.float32
        )
        quad_term = lax.dot_general(
            quad_weight,
            proj_power,
            (((1,), (1,)), ((), ())),
            precision=lax.Precision.HIGHEST,
            preferred_element_type=jnp.float32,
        )
        return -(norm_term[:, None, None] - 2.0 * cross_term + quad_term[:, None, :]) * score_scale

    members = (
        lax.all_gather(images, "blk", axis=0, tiled=True),
        lax.all_gather(ctf_group, "blk", axis=0, tiled=True),
        lax.all_gather(shift_offsets, "blk", axis=0, tiled=True),
        lax.all_gather(shell_limit, "blk", axis=0, tiled=True),
    )
    row_count = members[0].shape[0]
    block_rows = block_shape(row_count)
    blocks = lax.map(score_block, split_rows(members, block_rows))
    scores = blocks.reshape((row_count,) + blocks.shape[2:])
    local_top = jnp.max(scores, axis=(1, 2))
    local_total = jnp.sum(jnp.exp(scores - local_top[:, None, None]), axis=(1, 2))
    score_top, exp_total = combined_all((local_top, local_total), "blk", combine_lse)
    log_total = score_top + jnp.log(exp_total)
    pieces = (
        lax.all_gather(images, "blk", axis=0, tiled=True),
        lax.all_gather(ctf_group, "blk", axis=0, tiled=True),
        lax.all_gather(shift_offsets, "blk", axis=0, tiled=True),
        lax.all_gather(shell_limit, "blk", axis=0, tiled=True),
    )
    row_count = pieces[0].shape[0]
    block_rows = block_shape(row_count)

    def add_block(carry, packed):
        member_block, score_block_values, log_block = packed
        weighted = block_terms(member_block)[0]
        posterior = jnp.exp(score_block_values - log_block[:, None, None]).astype(jnp.bfloat16)
        contrib = lax.dot_general(
            posterior, weighted, (((0, 1), (0, 1)), ((), ())), preferred_element_type=jnp.float32
        )
        return (carry + contrib, None)

    zero_slices = jnp.zeros((candidates, full_width), jnp.float32)
    packed_scores = split_rows((scores, log_total), block_rows)
    summed, unused_out = lax.scan(
        add_block, zero_slices, (split_rows(pieces, block_rows), packed_scores[0], packed_scores[1])
    )
    slices = (summed * (candidates / particles_dev)).reshape(batch_count, orient_dev, full_width)
    own_start = lax.axis_index("blk") * particles_dev
    own_top = lax.dynamic_slice_in_dim(score_top, own_start, particles_dev, 0)
    own_log = lax.dynamic_slice_in_dim(log_total, own_start, particles_dev, 0)
    best_posterior = jnp.exp(own_top - own_log)
    return (slices, best_posterior, own_log)


def solution(mesh):
    in_specs = (
        P(None, ("groups", "blk"), None),
        P(("groups", "blk"), None),
        P(("groups", "blk")),
        P(("groups", "blk"), None, None),
        P(("groups", "blk")),
        P("groups", None),
        P("groups", None),
    )
    out_specs = (P(None, ("groups", "blk"), None), P(("groups", "blk")), P(("groups", "blk")))
    return jax.shard_map(local, mesh=mesh, in_specs=in_specs, out_specs=out_specs, check_vma=False)
```

profile of v0, /device:TPU:0, one launch (start us, length us, event | category | flops | bytes accessed | tf_op | source)
XLA Modules:
  0.0 127.0 jit_solution(18370479021721928491)
XLA Ops:
  0.6 0.0 copy-start
  0.6 23.6 %all_gather.31 = s32[32,9,2]{1,2,0:T(2,128)S(1)} all-gather(s32[2,9,2]{1,2,0:T(2,128)} %param.12), channel_id=1, replica_groups=mesh['groups'=2,'blk'=16] {'blk'}, dimensions={0}, use_global_device_ids=true | all-gather | bytes 2448 | tf_op jit(solution)/shard_map/all_gather | solution.py:145
  24.2 0.1 copy.14
  24.3 0.1 copy.13
  24.4 1.2 fusion.32
  25.6 7.2 %multiply_subtract_fusion = (f32[32,9,64,64]{3,2,0,1:T(8,128)}, f32[32,9,64,64]{3,2,0,1:T(8,128)}) fusion(f32[32,9,64]{2,0,1:T(8,128)S(1)} %get-tuple-element.134, f32[32,9,64]{2,0,1:T(8,128)S(1)} %get-tuple-element.140, f32[32,9,64]{2,0,1:T(8,128)S(1)} %get-tuple-element.133, f32[32,9,64]{2,0,1:T(8,128)S(1)} %get-tuple-element.141), kind=kLoop, calls=%fused_computation.8 | loop fusion | flops 7077888 | bytes 9732096 | tf_op jit(solution)/shard_map/while/body/eval_jaxpr/sub | solution.py:37
  32.8 8.3 %add.127 = f32[32,9,4096]{2,0,1:T(8,128)} reshape(f32[32,9,64,64]{3,2,0,1:T(8,128)} %get-tuple-element.126) | data formatting | bytes 9437184 | tf_op jit(solution)/shard_map/while/body/eval_jaxpr/add | solution.py:38
  41.1 0.0 copy-start.2
  41.1 8.4 %sub.78 = f32[32,9,4096]{2,0,1:T(8,128)} reshape(f32[32,9,64,64]{3,2,0,1:T(8,128)} %get-tuple-element.125) | data formatting | bytes 9437184 | tf_op jit(solution)/shard_map/while/body/eval_jaxpr/sub | solution.py:37
  49.5 18.8 %all-gather.2 = bf16[16,2,8192]{2,1,0:T(2,128)(2,1)S(1)} all-gather(bf16[1,2,8192]{2,1,0:T(2,128)(2,1)S(1)} %bitcast.43), channel_id=1, replica_groups=mesh['groups'=2,'blk'=16] {'blk'}, dimensions={0}, use_global_device_ids=true | all-gather | bytes 557056 | tf_op jit(solution)/shard_map/all_gather | solution.py:143
  68.3 0.2 reshape.156
  68.5 0.9 slice_convert_fusion.1
  69.4 0.6 dynamic-slice.6
  70.7 0.2 dynamic-update-slice
  70.9 0.2 dynamic-update-slice.1
  71.1 9.5 %all-reduce.4 = (s32[32]{0:T(128)S(1)}, s32[32]{0:T(128)S(1)}) all-reduce(s32[32]{0:T(128)S(1)} %dynamic-update-slice, s32[32]{0:T(128)S(1)} %dynamic-update-slice.1), channel_id=1, replica_groups=mesh['groups'=2,'blk'=16] {'blk'}, use_global_device_ids=true, to_apply=%add | all-reduce | flops 64 | bytes 512
  80.6 0.4 fusion.46
  81.1 0.6 multiply_reduce_fusion
  81.7 4.7 %multiply_convert_fusion.1 = (bf16[32,9,4096]{2,0,1:T(8,128)(2,1)S(1)}, bf16[32,9,4096]{2,0,1:T(8,128)(2,1)S(1)}) fusion(f32[32,9,4096]{2,0,1:T(8,128)} %add.127, f32[32,9,4096]{2,0,1:T(8,128)} %sub.78, f32[32,4096]{1,0:T(8,128)} %get-tuple-element.130, f32[32,4096]{1,0:T(8,128)S(1)} %get-tuple-element.129, f32[32,4096]{1,0:T(8,128)S(1)} %get-tuple-element.128), kind=kLoop, calls=%fused_computation.13 | loop fusion | flops 11796480 | bytes 15728640 | tf_op jit(solution)/shard_map/convert
  86.4 0.6 fusion.12
  87.0 3.5 %fusion.53 = (f32[32]{0:T(128)S(1)}, f32[32,9,32]{0,2,1:T(8,128)S(1)}) fusion(f32[32,32]{0,1:T(8,128)S(1)} %fusion.12, bf16[32,8192,1]{1,0,2:T(8,128)(2,1)S(1)} %bitcast.40, bf16[32,9,4096]{2,0,1:T(8,128)(2,1)S(1)} %get-tuple-element.124, bf16[32,9,4096]{2,0,1:T(8,128)(2,1)S(1)} %get-tuple-element.123, f32[32]{0:T(128)S(1)} %get-tuple-element.127), kind=kOutput, calls=%fused_computation.82 | convolution fusion | flops 160487392 | bytes 5284096 | tf_op jit(solution)/shard_map/while/body/eval_jaxpr/dot_general | solution.py:116
  91.2 0.2 dynamic-update-slice.2
  91.4 0.1 exponential_reduce_fusion
  91.5 0.2 dynamic-update-slice.3
  91.7 30.1 %all-reduce.5 = (f32[512]{0:T(512)S(1)}, f32[512]{0:T(512)S(1)}) all-reduce(f32[512]{0:T(512)S(1)} %dynamic-update-slice.2, f32[512]{0:T(512)S(1)} %dynamic-update-slice.3), channel_id=2, replica_groups=mesh['groups'=2,'blk'=16] {'blk'}, use_global_device_ids=true, to_apply=%add.2 | all-reduce | flops 1024 | bytes 8192
  121.8 0.1 slice.54
  121.9 0.1 reshape.141
  122.0 0.1 slice.55
  122.0 0.1 reshape.142
  122.1 0.6 while.2
  122.7 3.6 %fusion.5 = f32[32,8192]{1,0:T(8,128)} fusion(bf16[32,9,4096]{2,0,1:T(8,128)(2,1)} %copy-done.1, bf16[32,9,4096]{2,0,1:T(8,128)(2,1)S(1)} %get-tuple-element.123, f32[32,9,32]{0,2,1:T(8,128)S(1)} %get-tuple-element.139, f32[32]{0:T(128)S(1)} %log_add_fusion), kind=kOutput, calls=%fused_computation.10 | convolution fusion | flops 160712704 | bytes 5804160 | tf_op jit(solution)/shard_map/while/body/eval_jaxpr/dot_general | solution.py:155
  126.4 0.6 subtract_exponential_fusion
  (40 shorter events, 0.5 us)
Async XLA Ops:
  0.6 80.4 %copy-start = (f32[16,4096]{1,0:T(8,128)S(1)}, f32[16,4096]{1,0:T(8,128)}, u32[]{:S(2)}) copy-start(f32[16,4096]{1,0:T(8,128)} %param.15) | copy-start | bytes 786436
  41.1 8.4 %copy-start.4 = (bf16[2,8192]{1,0:T(2,128)(2,1)S(1)}, bf16[2,8192]{1,0:T(2,128)(2,1)}, u32[]{:S(2)}) copy-start(bf16[2,8192]{1,0:T(2,128)(2,1)} %param.10) | copy-start | bytes 98308
  41.1 28.3 %copy-start.7 = (u32[32]{0:T(128)S(1)}, u32[32]{0:T(128)}, u32[]{:S(2)}) copy-start(u32[32]{0:T(128)} %constant.138) | copy-start | bytes 388
  41.1 29.5 %copy-start.5 = (s32[2]{0:T(128)S(1)}, s32[2]{0:T(128)}, u32[]{:S(2)}) copy-start(s32[2]{0:T(128)} %param.13) | copy-start | bytes 28
  41.1 29.8 %copy-start.6 = (s32[2]{0:T(128)S(1)}, s32[2]{0:T(128)}, u32[]{:S(2)}) copy-start(s32[2]{0:T(128)} %param.11) | copy-start | bytes 28
  41.1 39.5 %copy-start.2 = (f32[16,4096]{1,0:T(8,128)S(1)}, f32[16,4096]{1,0:T(8,128)}, u32[]{:S(2)}) copy-start(f32[16,4096]{1,0:T(8,128)} %param.14) | copy-start | bytes 786436
  81.7 4.7 %copy-start.3 = (bf16[2,16,8192]{2,1,0:T(8,128)(2,1)S(1)}, bf16[2,16,8192]{2,1,0:T(8,128)(2,1)}, u32[]{:S(2)}) copy-start(bf16[2,16,8192]{2,1,0:T(8,128)(2,1)} %param.9) | copy-start | bytes 1572868
  86.3 4.2 %copy-start.1 = (bf16[32,9,4096]{2,0,1:T(8,128)(2,1)}, bf16[32,9,4096]{2,0,1:T(8,128)(2,1)S(1)}, u32[]{:S(2)}) copy-start(bf16[32,9,4096]{2,0,1:T(8,128)(2,1)S(1)} %get-tuple-element.124) | copy-start | bytes 7077892
where the time goes:
time: 127 us
  blocking collectives  81.9 us (64%)
  local copies, waits for them, and re-layouts  18.9 us (15%)
  other arithmetic  15 us (12%)
  matrix products  8.79 us (7%)
  between operations  2.1 us (2%)
    unnamed x2, blocking collectives  39.5 us
    all_gather x1, blocking collectives, local(): lax.all_gather(shift_offsets, 'blk', axis=0, tiled=True)  23.6 us
    all_gather x1, blocking collectives, local(): lax.all_gather(images, 'blk', axis=0, tiled=True)  18.8 us
    sub x1, local copies, waits for them, and re-layouts, shift_factors(): cosine = cosine_x * cosine_y - sine_x * sine_y  8.36 us
    add x1, local copies, waits for them, and re-layouts, shift_factors(): sine_part = sine_x * cosine_y + cosine_x * sine_y  8.32 us
    sub x1, other arithmetic, shift_factors(): cosine = cosine_x * cosine_y - sine_x * sine_y  7.17 us
    another operation x1, other arithmetic  4.66 us
    dot_general x1, matrix products, add_block(): lax.dot_general(posterior, weighted, (((0, 1), (0, 1)), ((), ())), prefer...  3.63 us

commit v1 on v0

--- a/solution.py
+++ b/solution.py
@@ -1,3 +1,4 @@
+import functools
 import math
 import jax
 import jax.numpy as jnp
@@ -6,6 +7,37 @@
 
 KY = 64
 IMG = 256
+
+
+def _perform_outputs(z_in, on_dim):
+    z_in = jnp.moveaxis(z_in, 0, on_dim)
+    part_now = z_in.shape
+    z_new = z_in.reshape(
+        *part_now[:on_dim], part_now[on_dim] * part_now[on_dim + 1], *part_now[on_dim + 2 :]
+    )
+    return z_new
+
+
+def _fix_slot(t0, axis_id, join_dim):
+    axis_total = lax.axis_size(axis_id)
+    runs = tuple(((w, (w + 1) % axis_total) for w in range(axis_total)))
+    arr_next, r2 = ([], [])
+    seen = tuple(((jj, c) for c, jj in runs))
+    kk = 0
+    while kk < axis_total - 1:
+        if kk % 2 == 0:
+            arr_next.append(lax.ppermute(arr_next[-1] if arr_next else t0, axis_id, runs))
+        else:
+            r2.append(lax.ppermute(r2[-1] if r2 else t0, axis_id, seen))
+        kk = kk + 1
+    front = jnp.stack([*arr_next[::-1], t0, *r2], 0)
+    opened = lax.axis_index(axis_id) - len(arr_next)
+    front = front[(jnp.arange(axis_total) - opened) % axis_total]
+    earlier = _perform_outputs(front, join_dim)
+    return earlier
+
+
+_derive_types = functools.partial(_fix_slot, axis_id="blk", join_dim=0)
 
 
 def combined_all(value, axis, join):
@@ -142,7 +174,7 @@
     pieces = (
         lax.all_gather(images, "blk", axis=0, tiled=True),
         lax.all_gather(ctf_group, "blk", axis=0, tiled=True),
-        lax.all_gather(shift_offsets, "blk", axis=0, tiled=True),
+        _derive_types(shift_offsets),
         lax.all_gather(shell_limit, "blk", axis=0, tiled=True),
     )
     row_count = pieces[0].shape[0]

time: 127 us -> 210 us (1.65)
  starting transfers between devices: 0 us -> 32.4 us
  local copies, waits for them, and re-layouts: 18.9 us -> 38.3 us
  other arithmetic: 15 us -> 28.4 us
  waiting for transfers between devices: 0 us -> 13.2 us
  blocking collectives: 81.9 us -> 84.6 us
    ppermute x0 -> x15, starting transfers between devices: none -> 32.4 us  [the longest x7 31.5 us: _fix_slot(): r2.append(lax.ppermute(r2[-1] if r2 else t0, axis_id, seen))]
    ppermute x0 -> x15, waiting for transfers between devices: none -> 13.2 us  [the longest x8 12.9 us: _fix_slot(): lax.ppermute(arr_next[-1] if arr_next else t0, axis_id, runs)]
    add x1 -> x2, local copies, waits for them, and re-layouts: 8.32 us -> 16.7 us  [shift_factors(): sine_part = sine_x * cosine_y + cosine_x * sine_y]
    sub x1 -> x2, local copies, waits for them, and re-layouts: 8.36 us -> 16.7 us  [shift_factors(): cosine = cosine_x * cosine_y - sine_x * sine_y]
    sub x1, other arithmetic: 7.17 us -> 13.9 us  [shift_factors(): cosine = cosine_x * cosine_y - sine_x * sine_y]
    another operation x1, other arithmetic: 4.66 us -> 9.76 us
    all_gather x1, blocking collectives: 18.8 us -> 23.8 us  [local(): lax.all_gather(images, 'blk', axis=0, tiled=True)]
    all_gather x1, blocking collectives: 23.6 us -> 19.6 us  [local(): lax.all_gather(shift_offsets, 'blk', axis=0, tiled=True)]
  transfers between devices with their start and end apart: 0 -> 15, of which waited for: 0 -> 7; matrix products, arithmetic and copies ran while one was open for 0% -> 4% of each run, Pallas kernels for 0% -> 0%
where the time goes in v1:
time: 210 us; the launch traced here: 209 us
  blocking collectives  84.6 us (40%)
  local copies, waits for them, and re-layouts  38.3 us (18%)
  starting transfers between devices  32.4 us (15%)
  other arithmetic  28.4 us (14%)
  waiting for transfers between devices  13.2 us (6%)
  matrix products  9.78 us (5%)
  between operations  2.19 us (1%)
    unnamed x2, blocking collectives  41.2 us
    ppermute x7, starting transfers between devices, _fix_slot(): r2.append(lax.ppermute(r2[-1] if r2 else t0, axis_id, seen))  31.5 us
    all_gather x1, blocking collectives, local(): lax.all_gather(images, 'blk', axis=0, tiled=True)  23.8 us
    all_gather x1, blocking collectives, local(): lax.all_gather(shift_offsets, 'blk', axis=0, tiled=True)  19.6 us
    sub x2, local copies, waits for them, and re-layouts, shift_factors(): cosine = cosine_x * cosine_y - sine_x * sine_y  16.7 us
    add x2, local copies, waits for them, and re-layouts, shift_factors(): sine_part = sine_x * cosine_y + cosine_x * sine_y  16.7 us
    sub x1, other arithmetic, shift_factors(): cosine = cosine_x * cosine_y - sine_x * sine_y  13.9 us
    ppermute x8, waiting for transfers between devices, _fix_slot(): lax.ppermute(arr_next[-1] if arr_next else t0, axis_id, runs)  12.9 us
  transfers between devices with their start and end apart: 15, of which 7 were waited for; matrix products, arithmetic and copies ran while one was open for 4% of the time, Pallas kernels for 0%

profile of v1, /device:TPU:0, one launch (start us, length us, event | category | flops | bytes accessed | tf_op | source)
XLA Modules:
  0.0 209.1 jit_solution(8113799220969559109)
XLA Ops:
  1.2 5.1 %collective-permute-start.8 = (s32[2,9,2]{1,2,0:T(2,128)}, s32[2,9,2]{1,2,0:T(2,128)S(1)}, u32[]{:S(2)}, u32[]{:S(2)}) collective-permute-start(s32[2,9,2]{1,2,0:T(2,128)} %param.12), channel_id=1, source_target_pairs={{1,0},{2,1},{3,2},{4,3},{5,4},{6,5},{7,6},{8,7},{9,8},{10,9},{11,1... | collective-permute-start | bytes 440 | tf_op jit(solution)/shard_map/ppermute | solution.py:31
  6.2 19.6 %all_gather.30 = s32[32,9,2]{1,2,0:T(2,128)S(1)} all-gather(s32[2,9,2]{1,2,0:T(2,128)} %param.12), channel_id=1, replica_groups=mesh['groups'=2,'blk'=16] {'blk'}, dimensions={0}, use_global_device_ids=true | all-gather | bytes 2448 | tf_op jit(solution)/shard_map/all_gather | solution.py:163
  26.8 1.2 dynamic-slice.6
  28.7 0.9 dynamic-update-slice
  29.5 0.8 dynamic-update-slice.1
  30.4 7.5 %all-reduce.4 = (s32[32]{0:T(128)S(1)}, s32[32]{0:T(128)S(1)}) all-reduce(s32[32]{0:T(128)S(1)} %dynamic-update-slice, s32[32]{0:T(128)S(1)} %dynamic-update-slice.1), channel_id=1, replica_groups=mesh['groups'=2,'blk'=16] {'blk'}, use_global_device_ids=true, to_apply=%add | all-reduce | flops 64 | bytes 512
  37.9 23.8 %all-gather.2 = bf16[16,2,8192]{2,1,0:T(2,128)(2,1)S(1)} all-gather(bf16[1,2,8192]{2,1,0:T(2,128)(2,1)} %bitcast.91), channel_id=1, replica_groups=mesh['groups'=2,'blk'=16] {'blk'}, dimensions={0}, use_global_device_ids=true | all-gather | bytes 557056 | tf_op jit(solution)/shard_map/all_gather | solution.py:175
  61.9 1.0 slice_convert_fusion.1
  63.6 1.4 fusion.75
  66.7 5.4 %collective-permute-done.1 = s32[2,9,2]{1,2,0:T(2,128)S(1)} collective-permute-done((s32[2,9,2]{1,2,0:T(2,128)S(1)}, s32[2,9,2]{1,2,0:T(2,128)S(1)}, u32[]{:S(2)}, u32[]{:S(2)}) %collective-permute-start.1) | collective-permute-done | bytes 176 | tf_op jit(solution)/shard_map/ppermute | solution.py:29
  72.0 4.4 %collective-permute-start.9 = (s32[2,9,2]{1,2,0:T(2,128)S(1)}, s32[2,9,2]{1,2,0:T(2,128)S(1)}, u32[]{:S(2)}, u32[]{:S(2)}) collective-permute-start(s32[2,9,2]{1,2,0:T(2,128)S(1)} %collective-permute-done.8), channel_id=1, source_target_pairs={{1,0},{2,1},{3,2},{4,3},{5,4},{6,5},{7,6},{8,7},{9,8},{10,9},{11,1... | collective-permute-start | bytes 440 | tf_op jit(solution)/shard_map/ppermute | solution.py:31
  76.5 1.3 collective-permute-done.2
  77.8 4.4 %collective-permute-start.10 = (s32[2,9,2]{1,2,0:T(2,128)S(1)}, s32[2,9,2]{1,2,0:T(2,128)S(1)}, u32[]{:S(2)}, u32[]{:S(2)}) collective-permute-start(s32[2,9,2]{1,2,0:T(2,128)S(1)} %collective-permute-done.9), channel_id=1, source_target_pairs={{1,0},{2,1},{3,2},{4,3},{5,4},{6,5},{7,6},{8,7},{9,8},{10,9},{11,1... | collective-permute-start | bytes 440 | tf_op jit(solution)/shard_map/ppermute | solution.py:31
  82.2 1.3 collective-permute-done.3
  83.5 4.4 %collective-permute-start.11 = (s32[2,9,2]{1,2,0:T(2,128)S(1)}, s32[2,9,2]{1,2,0:T(2,128)S(1)}, u32[]{:S(2)}, u32[]{:S(2)}) collective-permute-start(s32[2,9,2]{1,2,0:T(2,128)S(1)} %collective-permute-done.10), channel_id=1, source_target_pairs={{1,0},{2,1},{3,2},{4,3},{5,4},{6,5},{7,6},{8,7},{9,8},{10,9},{11,1... | collective-permute-start | bytes 440 | tf_op jit(solution)/shard_map/ppermute | solution.py:31
  87.9 1.3 collective-permute-done.4
  89.2 4.4 %collective-permute-start.12 = (s32[2,9,2]{1,2,0:T(2,128)S(1)}, s32[2,9,2]{1,2,0:T(2,128)S(1)}, u32[]{:S(2)}, u32[]{:S(2)}) collective-permute-start(s32[2,9,2]{1,2,0:T(2,128)S(1)} %collective-permute-done.11), channel_id=1, source_target_pairs={{1,0},{2,1},{3,2},{4,3},{5,4},{6,5},{7,6},{8,7},{9,8},{10,9},{11,1... | collective-permute-start | bytes 440 | tf_op jit(solution)/shard_map/ppermute | solution.py:31
  93.6 1.3 collective-permute-done.5
  94.9 4.4 %collective-permute-start.13 = (s32[2,9,2]{1,2,0:T(2,128)S(1)}, s32[2,9,2]{1,2,0:T(2,128)S(1)}, u32[]{:S(2)}, u32[]{:S(2)}) collective-permute-start(s32[2,9,2]{1,2,0:T(2,128)S(1)} %collective-permute-done.12), channel_id=1, source_target_pairs={{1,0},{2,1},{3,2},{4,3},{5,4},{6,5},{7,6},{8,7},{9,8},{10,9},{11,1... | collective-permute-start | bytes 440 | tf_op jit(solution)/shard_map/ppermute | solution.py:31
  99.3 1.3 collective-permute-done.6
  100.6 4.4 %collective-permute-start.14 = (s32[2,9,2]{1,2,0:T(2,128)S(1)}, s32[2,9,2]{1,2,0:T(2,128)S(1)}, u32[]{:S(2)}, u32[]{:S(2)}) collective-permute-start(s32[2,9,2]{1,2,0:T(2,128)S(1)} %collective-permute-done.13), channel_id=1, source_target_pairs={{1,0},{2,1},{3,2},{4,3},{5,4},{6,5},{7,6},{8,7},{9,8},{10,9},{11,1... | collective-permute-start | bytes 440 | tf_op jit(solution)/shard_map/ppermute | solution.py:31
  105.0 1.3 collective-permute-done.7
  107.9 1.2 fusion.61
  109.1 13.9 %multiply_subtract_fusion = (f32[32,9,64,64]{3,2,0,1:T(8,128)}, f32[32,9,64,64]{3,2,0,1:T(8,128)}, f32[32,9,64,64]{3,2,0,1:T(8,128)}, f32[32,9,64,64]{3,2,0,1:T(8,128)}) fusion(f32[32,9,64]{2,0,1:T(8,128)S(1)} %get-tuple-element.149, f32[32,9,64]{2,0,1:T(8,128)S(1)} %get-tuple-element.148, f32[32,9,64]{2,0,1:T(8,128)S(1)} %get-tuple-element.150, ...), kind=kLoop, calls=%fused_computation.9 | loop fusion | flops 14155776 | bytes 19464192 | tf_op jit(solution)/shard_map/while/body/eval_jaxpr/sub | solution.py:69
  123.1 8.3 %add.177 = f32[32,9,4096]{2,0,1:T(8,128)} reshape(f32[32,9,64,64]{3,2,0,1:T(8,128)} %get-tuple-element.154) | data formatting | bytes 9437184 | tf_op jit(solution)/shard_map/while/body/eval_jaxpr/add | solution.py:70
  131.4 8.3 %add.188 = f32[32,9,4096]{2,0,1:T(8,128)} reshape(f32[32,9,64,64]{3,2,0,1:T(8,128)} %get-tuple-element.132) | data formatting | bytes 9437184 | tf_op jit(solution)/shard_map/while/body/eval_jaxpr/add | solution.py:70
  139.7 8.3 %sub.104 = f32[32,9,4096]{2,0,1:T(8,128)} reshape(f32[32,9,64,64]{3,2,0,1:T(8,128)} %get-tuple-element.155) | data formatting | bytes 9437184 | tf_op jit(solution)/shard_map/while/body/eval_jaxpr/sub | solution.py:69
  148.1 8.3 %sub.115 = f32[32,9,4096]{2,0,1:T(8,128)} reshape(f32[32,9,64,64]{3,2,0,1:T(8,128)} %get-tuple-element.131) | data formatting | bytes 9437184 | tf_op jit(solution)/shard_map/while/body/eval_jaxpr/sub | solution.py:69
  156.4 9.8 %multiply_convert_fusion.3 = (bf16[32,9,4096]{2,0,1:T(8,128)(2,1)S(1)}, bf16[32,9,4096]{2,0,1:T(8,128)(2,1)S(1)}, bf16[32,9,4096]{2,0,1:T(8,128)(2,1)S(1)}, bf16[32,9,4096]{2,0,1:T(8,128)(2,1)}) fusion(f32[32,9,4096]{2,0,1:T(8,128)} %add.177, f32[32,9,4096]{2,0,1:T(8,128)} %sub.104, f32[32,4096]{1,0:T(8,128)} %get-tuple-element.136, ...), kind=kLoop, calls=%fused_computation.24 | loop fusion | flops 23592960 | bytes 29884416 | tf_op jit(solution)/shard_map/convert.2
  166.2 3.5 %fusion.85 = (f32[32]{0:T(128)S(1)}, f32[32,9,32]{0,2,1:T(8,128)S(1)}) fusion(f32[32,32]{0,1:T(8,128)S(1)} %fusion.28, bf16[32,8192,1]{1,0,2:T(8,128)(2,1)S(1)} %bitcast.86, bf16[32,9,4096]{2,0,1:T(8,128)(2,1)S(1)} %get-tuple-element.124, bf16[32,9,4096]{2,0,1:T(8,128)(2,1)S(1)} %get-tuple-element.123, f32[32]{0:T(128)S(1)} %get-tuple-element.133), kind=kOutput, calls=%fused_computation.137 | convolution fusion | flops 160487392 | bytes 5284096 | tf_op jit(solution)/shard_map/while/body/eval_jaxpr/dot_general | solution.py:148
  170.2 33.7 %all-reduce.5 = (f32[512]{0:T(512)S(1)}, f32[512]{0:T(512)S(1)}) all-reduce(f32[512]{0:T(512)S(1)} %dynamic-update-slice.2, f32[512]{0:T(512)S(1)} %dynamic-update-slice.3), channel_id=2, replica_groups=mesh['groups'=2,'blk'=16] {'blk'}, use_global_device_ids=true, to_apply=%add.2 | all-reduce | flops 1024 | bytes 8192
  205.5 3.6 %fusion.5 = f32[32,8192]{1,0:T(8,128)} fusion(bf16[32,9,4096]{2,0,1:T(8,128)(2,1)S(1)} %get-tuple-element.127, bf16[32,9,4096]{2,0,1:T(8,128)(2,1)} %get-tuple-element.128, f32[32,9,32]{0,2,1:T(8,128)S(1)} %get-tuple-element.153, f32[32]{0:T(128)S(1)} %log_add_fusion), kind=kOutput, calls=%fused_computation.13 | convolution fusion | flops 160712704 | bytes 5804160 | tf_op jit(solution)/shard_map/while/body/eval_jaxpr/dot_general | solution.py:187
  (90 shorter events, 7.6 us)
Async XLA Ops:
  0.6 64.3 %copy-start = (f32[16,4096]{1,0:T(8,128)S(1)}, f32[16,4096]{1,0:T(8,128)}, u32[]{:S(2)}) copy-start(f32[16,4096]{1,0:T(8,128)} %param.15) | copy-start | bytes 786436
  0.6 105.7 %copy-start.4 = (s32[2,9,2]{1,2,0:T(2,128)S(1)}, s32[2,9,2]{1,2,0:T(2,128)}, u32[]{:S(2)}) copy-start(s32[2,9,2]{1,2,0:T(2,128)} %param.12) | copy-start | bytes 436
  0.7 64.9 %copy-start.2 = (bf16[2,16,8192]{2,1,0:T(8,128)(2,1)S(1)}, bf16[2,16,8192]{2,1,0:T(8,128)(2,1)}, u32[]{:S(2)}) copy-start(bf16[2,16,8192]{2,1,0:T(8,128)(2,1)} %param.9) | copy-start | bytes 1572868
  0.7 65.6 %collective-permute-start = (s32[2,9,2]{1,2,0:T(2,128)}, s32[2,9,2]{1,2,0:T(2,128)S(1)}, u32[]{:S(2)}, u32[]{:S(2)}) collective-permute-start(s32[2,9,2]{1,2,0:T(2,128)} %param.12), channel_id=1, source_target_pairs={{0,1},{1,2},{2,3},{3,4},{4,5},{5,6},{6,7},{7,8},{8,9},{9,10},{10,1... | collective-permute-start | bytes 440 | tf_op jit(solution)/shard_map/ppermute | solution.py:29
  1.2 70.8 %collective-permute-start.8 = (s32[2,9,2]{1,2,0:T(2,128)}, s32[2,9,2]{1,2,0:T(2,128)S(1)}, u32[]{:S(2)}, u32[]{:S(2)}) collective-permute-start(s32[2,9,2]{1,2,0:T(2,128)} %param.12), channel_id=1, source_target_pairs={{1,0},{2,1},{3,2},{4,3},{5,4},{6,5},{7,6},{8,7},{9,8},{10,9},{11,1... | collective-permute-start | bytes 440 | tf_op jit(solution)/shard_map/ppermute | solution.py:31
  66.3 5.8 %collective-permute-start.1 = (s32[2,9,2]{1,2,0:T(2,128)S(1)}, s32[2,9,2]{1,2,0:T(2,128)S(1)}, u32[]{:S(2)}, u32[]{:S(2)}) collective-permute-start(s32[2,9,2]{1,2,0:T(2,128)S(1)} %collective-permute-done), channel_id=1, source_target_pairs={{0,1},{1,2},{2,3},{3,4},{4,5},{5,6},{6,7},{7,8},{8,9},{9,10},{10,1... | collective-permute-start | bytes 440 | tf_op jit(solution)/shard_map/ppermute | solution.py:29
  72.0 5.7 %collective-permute-start.2 = (s32[2,9,2]{1,2,0:T(2,128)S(1)}, s32[2,9,2]{1,2,0:T(2,128)S(1)}, u32[]{:S(2)}, u32[]{:S(2)}) collective-permute-start(s32[2,9,2]{1,2,0:T(2,128)S(1)} %collective-permute-done.1), channel_id=1, source_target_pairs={{0,1},{1,2},{2,3},{3,4},{4,5},{5,6},{6,7},{7,8},{8,9},{9,10},{10,1... | collective-permute-start | bytes 440 | tf_op jit(solution)/shard_map/ppermute | solution.py:29
  72.0 5.8 %collective-permute-start.9 = (s32[2,9,2]{1,2,0:T(2,128)S(1)}, s32[2,9,2]{1,2,0:T(2,128)S(1)}, u32[]{:S(2)}, u32[]{:S(2)}) collective-permute-start(s32[2,9,2]{1,2,0:T(2,128)S(1)} %collective-permute-done.8), channel_id=1, source_target_pairs={{1,0},{2,1},{3,2},{4,3},{5,4},{6,5},{7,6},{8,7},{9,8},{10,9},{11,1... | collective-permute-start | bytes 440 | tf_op jit(solution)/shard_map/ppermute | solution.py:31
  77.7 5.7 %collective-permute-start.3 = (s32[2,9,2]{1,2,0:T(2,128)S(1)}, s32[2,9,2]{1,2,0:T(2,128)S(1)}, u32[]{:S(2)}, u32[]{:S(2)}) collective-permute-start(s32[2,9,2]{1,2,0:T(2,128)S(1)} %collective-permute-done.2), channel_id=1, source_target_pairs={{0,1},{1,2},{2,3},{3,4},{4,5},{5,6},{6,7},{7,8},{8,9},{9,10},{10,1... | collective-permute-start | bytes 440 | tf_op jit(solution)/shard_map/ppermute | solution.py:29
  77.8 5.7 %collective-permute-start.10 = (s32[2,9,2]{1,2,0:T(2,128)S(1)}, s32[2,9,2]{1,2,0:T(2,128)S(1)}, u32[]{:S(2)}, u32[]{:S(2)}) collective-permute-start(s32[2,9,2]{1,2,0:T(2,128)S(1)} %collective-permute-done.9), channel_id=1, source_target_pairs={{1,0},{2,1},{3,2},{4,3},{5,4},{6,5},{7,6},{8,7},{9,8},{10,9},{11,1... | collective-permute-start | bytes 440 | tf_op jit(solution)/shard_map/ppermute | solution.py:31
  83.4 5.7 %collective-permute-start.4 = (s32[2,9,2]{1,2,0:T(2,128)S(1)}, s32[2,9,2]{1,2,0:T(2,128)S(1)}, u32[]{:S(2)}, u32[]{:S(2)}) collective-permute-start(s32[2,9,2]{1,2,0:T(2,128)S(1)} %collective-permute-done.3), channel_id=1, source_target_pairs={{0,1},{1,2},{2,3},{3,4},{4,5},{5,6},{6,7},{7,8},{8,9},{9,10},{10,1... | collective-permute-start | bytes 440 | tf_op jit(solution)/shard_map/ppermute | solution.py:29
  83.5 5.7 %collective-permute-start.11 = (s32[2,9,2]{1,2,0:T(2,128)S(1)}, s32[2,9,2]{1,2,0:T(2,128)S(1)}, u32[]{:S(2)}, u32[]{:S(2)}) collective-permute-start(s32[2,9,2]{1,2,0:T(2,128)S(1)} %collective-permute-done.10), channel_id=1, source_target_pairs={{1,0},{2,1},{3,2},{4,3},{5,4},{6,5},{7,6},{8,7},{9,8},{10,9},{11,1... | collective-permute-start | bytes 440 | tf_op jit(solution)/shard_map/ppermute | solution.py:31
  89.1 5.7 %collective-permute-start.5 = (s32[2,9,2]{1,2,0:T(2,128)S(1)}, s32[2,9,2]{1,2,0:T(2,128)S(1)}, u32[]{:S(2)}, u32[]{:S(2)}) collective-permute-start(s32[2,9,2]{1,2,0:T(2,128)S(1)} %collective-permute-done.4), channel_id=1, source_target_pairs={{0,1},{1,2},{2,3},{3,4},{4,5},{5,6},{6,7},{7,8},{8,9},{9,10},{10,1... | collective-permute-start | bytes 440 | tf_op jit(solution)/shard_map/ppermute | solution.py:29
  89.2 5.7 %collective-permute-start.12 = (s32[2,9,2]{1,2,0:T(2,128)S(1)}, s32[2,9,2]{1,2,0:T(2,128)S(1)}, u32[]{:S(2)}, u32[]{:S(2)}) collective-permute-start(s32[2,9,2]{1,2,0:T(2,128)S(1)} %collective-permute-done.11), channel_id=1, source_target_pairs={{1,0},{2,1},{3,2},{4,3},{5,4},{6,5},{7,6},{8,7},{9,8},{10,9},{11,1... | collective-permute-start | bytes 440 | tf_op jit(solution)/shard_map/ppermute | solution.py:31
  94.8 5.7 %collective-permute-start.6 = (s32[2,9,2]{1,2,0:T(2,128)S(1)}, s32[2,9,2]{1,2,0:T(2,128)S(1)}, u32[]{:S(2)}, u32[]{:S(2)}) collective-permute-start(s32[2,9,2]{1,2,0:T(2,128)S(1)} %collective-permute-done.5), channel_id=1, source_target_pairs={{0,1},{1,2},{2,3},{3,4},{4,5},{5,6},{6,7},{7,8},{8,9},{9,10},{10,1... | collective-permute-start | bytes 440 | tf_op jit(solution)/shard_map/ppermute | solution.py:29
  94.9 5.7 %collective-permute-start.13 = (s32[2,9,2]{1,2,0:T(2,128)S(1)}, s32[2,9,2]{1,2,0:T(2,128)S(1)}, u32[]{:S(2)}, u32[]{:S(2)}) collective-permute-start(s32[2,9,2]{1,2,0:T(2,128)S(1)} %collective-permute-done.12), channel_id=1, source_target_pairs={{1,0},{2,1},{3,2},{4,3},{5,4},{6,5},{7,6},{8,7},{9,8},{10,9},{11,1... | collective-permute-start | bytes 440 | tf_op jit(solution)/shard_map/ppermute | solution.py:31
  100.6 5.7 %collective-permute-start.7 = (s32[2,9,2]{1,2,0:T(2,128)S(1)}, s32[2,9,2]{1,2,0:T(2,128)S(1)}, u32[]{:S(2)}, u32[]{:S(2)}) collective-permute-start(s32[2,9,2]{1,2,0:T(2,128)S(1)} %collective-permute-done.6), channel_id=1, source_target_pairs={{0,1},{1,2},{2,3},{3,4},{4,5},{5,6},{6,7},{7,8},{8,9},{9,10},{10,1... | collective-permute-start | bytes 440 | tf_op jit(solution)/shard_map/ppermute | solution.py:29
  100.6 5.8 %collective-permute-start.14 = (s32[2,9,2]{1,2,0:T(2,128)S(1)}, s32[2,9,2]{1,2,0:T(2,128)S(1)}, u32[]{:S(2)}, u32[]{:S(2)}) collective-permute-start(s32[2,9,2]{1,2,0:T(2,128)S(1)} %collective-permute-done.13), channel_id=1, source_target_pairs={{1,0},{2,1},{3,2},{4,3},{5,4},{6,5},{7,6},{8,7},{9,8},{10,9},{11,1... | collective-permute-start | bytes 440 | tf_op jit(solution)/shard_map/ppermute | solution.py:31
  156.4 9.8 %copy-start.3 = (bf16[2,16,8192]{2,1,0:T(8,128)(2,1)S(1)}, bf16[2,16,8192]{2,1,0:T(8,128)(2,1)}, u32[]{:S(2)}) copy-start(bf16[2,16,8192]{2,1,0:T(8,128)(2,1)} %param.9) | copy-start | bytes 1572868
  166.2 42.9 %copy-start.1 = (f32[16,4096]{1,0:T(8,128)S(1)}, f32[16,4096]{1,0:T(8,128)}, u32[]{:S(2)}) copy-start(f32[16,4096]{1,0:T(8,128)} %param.15) | copy-start | bytes 786436
